TPU v7x, 32 devices: a whole 2x2x4 slice. The times are simulated.
32 devices in a mesh: groups: 2 (over y), tensor: 4 (over z), dp: 2 (over x), pipe: 2 (over core).
Axes of the slice: x: 2, y: 2, z: 4, core: 2. Of those that a mesh axis runs over, the one named last changes fastest.
Arguments:
- activations: bfloat16 [4096, 8192], P(('groups', 'dp', 'pipe'), 'tensor'), parts along dimension 0, may hold values from -6 to 6
- query_weight: bfloat16 [8192, 8192], P(('dp', 'pipe'), 'tensor'), may hold values from -0.0625 to 0.0625
- offsets: int32 [66], P('groups'), parts along dimension 0, may hold values from 0 to 2048, as said below
- request_adapter: int32 [64], P('groups'), parts along dimension 0, may hold values from 0 to 1999, as said below
- page_table: int32 [4000], P('groups'), parts along dimension 0, may hold values from -1 to 63, as said below
- shrink_pages: bfloat16 [128, 8192, 64], P(('groups', 'dp', 'pipe'), 'tensor'), parts along dimension 0, may hold values from -0.0625 to 0.0625
- expand_pages: bfloat16 [128, 64, 8192], P(('groups', 'dp', 'pipe'), None, 'tensor'), parts along dimension 0, may hold values from -0.75 to 0.75
Outputs:
- queries: bfloat16 [4096, 8192], P(('groups', 'dp', 'pipe'), 'tensor'), parts along dimension 0
There are 2 independent parts, one for each index of `groups`. A program takes and returns all parts, laid end to end along the dimension named above; an argument that names none is the same for every part. Nothing has to cross between parts.
Inputs may be any that keep to these rules, and one draw needn't show every extreme that they name: `offsets`: rises from 0 to 2048; every request holds 32 tokens or more, so the rows of one device meet at most 17 requests, and in every draw the rows of some device meet exactly 17. `request_adapter`: the requests use different resident adapters; request r sits on a page of the page shard (r + c) mod (number of devices along dp and pipe) for a constant c of the draw, so the rows of one device use at most 5 pages of any one shard, a bound that some device reaches in every draw. `page_table`: exactly 64 adapters are resident, each on its own page.
All inputs are finite; a program needn't handle non-finite values.
Results may differ from a plain program's by a relative error of at most 0.0065.
Values may be sent and summed in bfloat16 or wider, within the bound.
A program may use at most 192 MiB of HBM per device.

v0:
```python
import jax
import jax.numpy as jnp
from jax import lax
from jax.experimental import pallas as pl
from jax.experimental.pallas import tpu as pltpu
from jax.sharding import PartitionSpec as P


def slot_table(offsets, request_adapter, page_table, first, rows, used):
    reqs = offsets.shape[0] - 1
    adapter_ids = jnp.arange(page_table.shape[0], dtype=jnp.int32)
    match = (request_adapter[:, None] == adapter_ids[None, :]).astype(jnp.int32)
    page_of_request = jnp.sum(match * page_table[None, :], axis=1)
    leading = jnp.sum((offsets[1:] <= first).astype(jnp.int32))
    wanted = leading + jnp.arange(used, dtype=jnp.int32)
    clipped = jnp.clip(wanted, 0, reqs - 1)
    valid = (wanted < reqs) & (offsets[clipped] < first + rows)
    return (leading, page_of_request[clipped], valid)


def token_select(positions, offsets, leading, used):
    request = jnp.sum((offsets[None, 1:] <= positions[:, None]).astype(jnp.int32), axis=1)
    slot_of = request - leading
    return (slot_of[:, None] == jnp.arange(used, dtype=jnp.int32)[None, :]).astype(jnp.float32)


def shrink_term(local, factors, select):
    scores = jnp.einsum("tf,kfr->tkr", local, factors, preferred_element_type=jnp.float32)
    return jnp.sum(select[:, :, None] * scores, axis=1)


def expand_term(shrunk, factors, select):
    spread = (select[:, :, None] * shrunk[:, None, :].astype(jnp.float32)).astype(jnp.bfloat16)
    return jnp.einsum("tkr,krc->tc", spread, factors, preferred_element_type=jnp.float32)


def body(
    activations, query_weight, offsets, request_adapter, page_table, shrink_pages, expand_pages
):
    rows = activations.shape[0]
    shards = lax.axis_size(("dp", "pipe"))
    reqs = offsets.shape[0] - 1
    shortest = rows * shards // (2 * reqs)
    used = (rows - 2) // shortest + 2
    here = lax.axis_index(("dp", "pipe"))
    first = here * rows
    positions = first + jnp.arange(rows, dtype=jnp.int32)
    leading, pages, valid = slot_table(offsets, request_adapter, page_table, first, rows, used)
    select = token_select(positions, offsets, leading, used)
    whole = lax.all_gather(activations, "tensor", axis=1, tiled=True)
    base = jnp.dot(
        whole,
        lax.all_gather(query_weight, ("dp", "pipe"), axis=0, tiled=True),
        preferred_element_type=jnp.float32,
    )
    shrink_all, expand_all = (
        lax.all_gather(shrink_pages, ("dp", "pipe"), axis=0, tiled=True),
        lax.all_gather(expand_pages, ("dp", "pipe"), axis=0, tiled=True),
    )
    shrink_used = jnp.take(shrink_all, pages, axis=0)
    expand_used = jnp.take(expand_all, pages, axis=0)
    partial_value = shrink_term(activations, shrink_used, select)
    shrunk = lax.psum(partial_value, "tensor").astype(jnp.bfloat16)
    added = expand_term(shrunk, expand_used, select)
    return (base + added).astype(jnp.bfloat16)


MESH = pl.DeviceIdType.MESH
LANES = 128
CHUNKS = 4
HALVES = 2


def relay_kernel(
    act, weight, shrink, expand, slots, out,
    xp, ab, wv, sv, ev, mv, part, rsb, sh, spread, cs, rc, sx, rx, ov,
    load_sem, own_send, own_recv, fwd_send, fwd_recv, xown_send, xown_recv,
    up_send, dn_send, flow_recv, rs_send, rs_recv, ag_send, ag_recv,
    cs_send, cs_recv, x_send, x_recv, out_sem,
):
    x, p, z = lax.axis_index("dp"), lax.axis_index("pipe"), lax.axis_index("tensor")
    nz = lax.axis_size("tensor")
    rows = act.shape[0]
    ch = rows // CHUNKS
    hf = rows // HALVES
    d = 2 * x + p
    core, other = {"pipe": 1 - p}, {"dp": 1 - x}
    origin = z == d

    def blk(k):
        return 2 * (x if k < 2 else 1 - x) + (p if k % 2 == 0 else 1 - p)

    def rcopy(src, dst, ss, rs, dev):
        return pltpu.make_async_remote_copy(
            src_ref=src, dst_ref=dst, send_sem=ss, recv_sem=rs, device_id=dev, device_id_type=MESH
        )

    def cr(c):
        return pl.ds(c * ch, ch)

    def hr(h):
        return pl.ds(h * hf, hf)

    loads = [
        pltpu.make_async_copy(act, xp.at[d], load_sem.at[0]),
        pltpu.make_async_copy(shrink, sv, load_sem.at[1]),
        pltpu.make_async_copy(slots, mv, load_sem.at[2]),
        pltpu.make_async_copy(weight, wv, load_sem.at[3]),
        pltpu.make_async_copy(expand, ev, load_sem.at[4]),
    ]
    for cp in loads:
        cp.start()
    barrier = pltpu.get_barrier_semaphore()
    for j in range(1, nz):
        pl.semaphore_signal(barrier, inc=1, device_id={"tensor": lax.rem(z + j, nz)}, device_id_type=MESH)
    pl.semaphore_signal(barrier, inc=1, device_id=core, device_id_type=MESH)
    pl.semaphore_signal(barrier, inc=1, device_id=other, device_id_type=MESH)
    pl.semaphore_wait(barrier, nz + 1)
    loads[0].wait()

    def own_x(c):
        s = xp.at[d, cr(c)]
        return rcopy(s, s, xown_send.at[c], xown_recv.at[c], other)

    def own_core(c):
        s = xp.at[d, cr(c)]
        return rcopy(s, s, own_send.at[c], own_recv.at[c], core)

    def fwd(c):
        s = xp.at[blk(2), cr(c)]
        return rcopy(s, s, fwd_send.at[c], fwd_recv.at[c], core)

    def flow(k, c, src, step):
        b = blk(k)
        sem = up_send if step == 1 else dn_send
        return rcopy(
            src.at[b, cr(c)], ab.at[b, cr(c)], sem.at[k, c], flow_recv.at[k, c], {"tensor": z + step}
        )

    up = (z >= d) & (z < nz - 1)
    dn = (z <= d) & (z > 0)

    def send_flow(k, c, src):
        @pl.when(up)
        def _():
            flow(k, c, src, 1).start()

        @pl.when(dn)
        def _():
            flow(k, c, src, -1).start()

    def relay(k, c):
        @pl.when(jnp.logical_not(origin))
        def _():
            s = ab.at[blk(k), cr(c)]
            rcopy(s, s, up_send.at[k, c], flow_recv.at[k, c], core).wait_recv()
            send_flow(k, c, ab)

    for c in range(CHUNKS):
        own_x(c).start()
        own_core(c).start()

        @pl.when(origin)
        def _():
            send_flow(0, c, xp)

    for c in range(CHUNKS):
        own_core(c).wait_recv()

        @pl.when(origin)
        def _():
            send_flow(1, c, xp)

        own_x(c).wait_recv()
        fwd(c).start()

        @pl.when(origin)
        def _():
            send_flow(2, c, xp)

        if c > 0:
            relay(0, c - 1)
            relay(1, c - 1)
        fwd(c).wait_recv()

        @pl.when(origin)
        def _():
            send_flow(3, c, xp)

    relay(0, CHUNKS - 1)
    relay(1, CHUNKS - 1)

    loads[1].wait()
    loads[2].wait()
    groups = sv.shape[1] // LANES

    def shrink_step(i, _):
        b, r = i // HALVES, pl.ds(pl.multiple_of((i % HALVES) * hf, hf), hf)
        scores = jnp.dot(xp[b, r, :], sv[...], preferred_element_type=jnp.float32)
        m = mv[b, r, :]
        total = jnp.zeros((hf, LANES), jnp.float32)
        for g in range(groups):
            total += jnp.where(m == 2 * g, scores[:, g * LANES:(g + 1) * LANES], 0.0)
        part[b, r, :] = total.astype(jnp.bfloat16)
        return 0

    lax.fori_loop(0, nz * HALVES, shrink_step, 0)

    def rs_copy(j):
        to = lax.rem(z + j, nz)
        return rcopy(part.at[to], rsb.at[j - 1], rs_send.at[j - 1], rs_recv.at[j - 1], {"tensor": to})

    def ag_copy(j):
        to = lax.rem(z + j, nz)
        return rcopy(sh.at[z], sh.at[z], ag_send.at[j - 1], ag_recv.at[j - 1], {"tensor": to})

    for j in range(1, nz):
        rs_copy(j).start()

    for c in range(1):
        relay(2, c)
        relay(3, c)
    for j in range(1, nz):
        rs_copy(j).wait_recv()
    total = part[z].astype(jnp.float32)
    for j in range(1, nz):
        total += rsb[j - 1].astype(jnp.float32)
    sh[z] = total.astype(jnp.bfloat16)
    for j in range(1, nz):
        ag_copy(j).start()
    relay(2, 1)
    relay(3, 1)
    for j in range(1, nz):
        ag_copy(j).wait_recv()
    loads[3].wait()
    loads[4].wait()

    @pl.when(origin)
    def _():
        cp = pltpu.make_async_copy(xp, ab, load_sem.at[5])
        cp.start()
        cp.wait()

    tile = min(512, wv.shape[1])

    def compute(k, h, emit):
        b = blk(k)
        m = mv[b, hr(h), :]
        s = sh[b, hr(h), :]
        for g in range(groups):
            spread[:, g * LANES:(g + 1) * LANES] = jnp.where(m == 2 * g, s, jnp.zeros_like(s))

        def step(n, _):
            cols = pl.ds(pl.multiple_of(n * tile, tile), tile)
            value = jnp.dot(ab[b, hr(h), :], wv[:, cols], preferred_element_type=jnp.float32)
            value += jnp.dot(spread[...], ev[:, cols], preferred_element_type=jnp.float32)
            emit(value, cols)
            return 0

        lax.fori_loop(0, wv.shape[1] // tile, step, 0)

    def core_copy(i, h):
        return rcopy(cs.at[i, hr(h)], rc.at[i, hr(h)], cs_send.at[i, h], cs_recv.at[i, h], core)

    def x_copy(h):
        return rcopy(sx.at[hr(h)], rx.at[hr(h)], x_send.at[h], x_recv.at[h], other)

    def out_copy(h):
        return pltpu.make_async_copy(ov.at[hr(h)], out.at[hr(h)], out_sem.at[h])

    def to_core(i, k, h):
        def emit(value, cols):
            cs[i, hr(h), cols] = value.astype(jnp.bfloat16)

        compute(k, h, emit)
        core_copy(i, h).start()

    def to_x(h):
        core_copy(1, h).wait_recv()

        def emit(value, cols):
            sx[hr(h), cols] = (value + rc[1, hr(h), cols].astype(jnp.float32)).astype(jnp.bfloat16)

        compute(2, h, emit)
        x_copy(h).start()

    for h in range(HALVES):
        if h > 0:
            for c in range(2 * h, 2 * h + 2):
                relay(2, c)
                relay(3, c)
        to_core(1, 3, h)
        if h == 0:
            to_core(0, 1, 0)
        to_x(h)
        if h == 0:
            to_core(0, 1, 1)

    for h in range(HALVES):
        core_copy(0, h).wait_recv()

        x_copy(h).wait_recv()

        def emit(value, cols):
            value += rc[0, hr(h), cols].astype(jnp.float32) + rx[hr(h), cols].astype(jnp.float32)
            ov[hr(h), cols] = value.astype(jnp.bfloat16)

        compute(0, h, emit)
        out_copy(h).start()

    for h in range(HALVES):
        out_copy(h).wait()
        core_copy(0, h).wait_send()
        core_copy(1, h).wait_send()
        x_copy(h).wait_send()
    for j in range(1, nz):
        rs_copy(j).wait_send()
        ag_copy(j).wait_send()
    for c in range(CHUNKS):
        own_x(c).wait_send()
        own_core(c).wait_send()
        fwd(c).wait_send()
    for k in range(4):
        for c in range(CHUNKS):

            @pl.when(up)
            def _():
                flow(k, c, ab, 1).wait_send()

            @pl.when(dn)
            def _():
                flow(k, c, ab, -1).wait_send()


def relay_body(
    activations, query_weight, offsets, request_adapter, page_table, shrink_pages, expand_pages
):
    rows, feats = activations.shape
    cols = query_weight.shape[1]
    shards = lax.axis_size(("dp", "pipe"))
    reqs = offsets.shape[0] - 1
    held, _, rank = shrink_pages.shape
    mine = reqs // shards
    shard = lax.axis_index(("dp", "pipe"))
    adapter_ids = jnp.arange(page_table.shape[0], dtype=jnp.int32)
    match = (request_adapter[:, None] == adapter_ids[None, :]).astype(jnp.int32)
    page_of_request = jnp.sum(match * page_table[None, :], axis=1)
    lead = (shard - page_of_request[0] // held + shards) % shards
    pages = page_of_request.reshape(mine, shards)
    hot = (jnp.arange(shards, dtype=jnp.int32) == lead).astype(jnp.int32)
    pages = jnp.clip(jnp.sum(pages * hot[None, :], axis=1) - shard * held, 0, held - 1)
    positions = jnp.arange(rows * shards, dtype=jnp.int32)
    request = jnp.sum((offsets[None, 1:] <= positions[:, None]).astype(jnp.int32), axis=1)
    slot = jnp.where(request % shards == lead, request // shards, -8)
    upper = (jnp.arange(LANES, dtype=jnp.int32) >= rank).astype(jnp.int32)
    slots = (slot[:, None] - upper[None, :]).reshape(shards, rows, LANES)
    shrink = jnp.take(shrink_pages, pages, axis=0).transpose(1, 0, 2).reshape(feats, mine * rank)
    expand = jnp.take(expand_pages, pages, axis=0).reshape(mine * rank, cols)
    bf, dma = jnp.bfloat16, pltpu.SemaphoreType.DMA
    hf = rows // HALVES
    nz = lax.axis_size("tensor")
    return pl.pallas_call(
        relay_kernel,
        out_shape=jax.ShapeDtypeStruct((rows, cols), bf),
        in_specs=[pl.BlockSpec(memory_space=pl.ANY)] * 5,
        out_specs=pl.BlockSpec(memory_space=pl.ANY),
        scratch_shapes=[
            pltpu.VMEM((shards, rows, feats), bf),
            pltpu.VMEM((shards, rows, feats), bf),
            pltpu.VMEM(query_weight.shape, bf),
            pltpu.VMEM(shrink.shape, bf),
            pltpu.VMEM(expand.shape, bf),
            pltpu.VMEM(slots.shape, jnp.int32),
            pltpu.VMEM((shards, rows, LANES), bf),
            pltpu.VMEM((nz - 1, rows, LANES), bf),
            pltpu.VMEM((shards, rows, LANES), bf),
            pltpu.VMEM((hf, mine * rank), bf),
            pltpu.VMEM((2, rows, cols), bf),
            pltpu.VMEM((2, rows, cols), bf),
            pltpu.VMEM((rows, cols), bf),
            pltpu.VMEM((rows, cols), bf),
            pltpu.VMEM((rows, cols), bf),
            dma((6,)),
            dma((CHUNKS,)), dma((CHUNKS,)), dma((CHUNKS,)), dma((CHUNKS,)), dma((CHUNKS,)), dma((CHUNKS,)),
            dma((4, CHUNKS)), dma((4, CHUNKS)), dma((4, CHUNKS)),
            dma((nz - 1,)), dma((nz - 1,)), dma((nz - 1,)), dma((nz - 1,)),
            dma((2, HALVES)), dma((2, HALVES)), dma((HALVES,)), dma((HALVES,)), dma((HALVES,)),
        ],
        compiler_params=pltpu.CompilerParams(
            collective_id=0, has_side_effects=True, vmem_limit_bytes=60 * 1024 * 1024
        ),
        cost_estimate=pl.CostEstimate(
            flops=2 * shards * rows * feats * cols, bytes_accessed=2 * feats * cols, transcendentals=0
        ),
    )(activations, query_weight, shrink, expand, slots)


def solution(mesh):
    small = mesh.shape["dp"] == 2 and mesh.shape["pipe"] == 2 and mesh.shape["tensor"] == 4
    return jax.shard_map(
        relay_body if small else body,
        mesh=mesh,
        in_specs=(
            P(("groups", "dp", "pipe"), "tensor"),
            P(("dp", "pipe"), "tensor"),
            P("groups"),
            P("groups"),
            P("groups"),
            P(("groups", "dp", "pipe"), "tensor", None),
            P(("groups", "dp", "pipe"), None, "tensor"),
        ),
        out_specs=P(("groups", "dp", "pipe"), "tensor"),
        check_vma=False,
    )
```

profile of v0, /device:TPU:0, one launch (start us, length us, event | category | flops | bytes accessed | tf_op | source)
XLA Modules:
  0.0 308.7 jit_solution(18028761119239354182)
XLA Ops:
  0.0 0.9 select_reduce_fusion
  1.1 0.7 slice.7
  1.8 0.1 reshape.93
  1.9 0.1 multiply_reduce_fusion
  2.1 0.1 broadcast_in_dim.38
  2.1 0.1 broadcast_in_dim.39
  2.2 0.1 convert_reduce_fusion
  2.4 1.3 broadcast_subtract_fusion.slots
  3.7 2.9 gather_fusion.1
  6.6 1.7 bitcast_select_fusion.expand
  8.3 2.9 gather_fusion
  11.2 1.6 broadcast_select_fusion
  12.7 3.9 %copy.10.shrink = bf16[2048,512]{1,0:T(8,128)(2,1)} copy(bf16[2048,512]{0,1:T(8,128)(2,1)} %bitcast.11) | data formatting | bytes 4194304 | tf_op jit(solution)/shard_map/reshape | solution.py:357
  16.7 288.8 %shard_map.73 = bf16[512,2048]{1,0:T(8,128)(2,1)} custom-call(bf16[512,2048]{1,0:T(8,128)(2,1)} %act.1, bf16[2048,2048]{1,0:T(8,128)(2,1)} %weight.1, bf16[2048,512]{1,0:T(8,128)(2,1)} %copy.10.shrink, bf16[512,2048]{1,0:T(8,128)(2,1)} %bitcast_select_fusion.expand, s32[4,512,128]{2,1,0:T(8,128)} %broadcast_subtract_fusion.slots), custom_call_target="tpu_custom_call" | custom-call | flops 17179869184 | bytes 8388608 | tf_op jit(solution)/shard_map/pallas_call | solution.py:362
  305.5 3.2 %copy.12 = bf16[512,2048]{1,0:T(8,128)(2,1)} copy(bf16[512,2048]{1,0:T(8,128)(2,1)} %shard_map.73) | data formatting | bytes 4194304
  (7 shorter events, 0.1 us)
where the time goes:
time: 309 us
  Pallas kernels  289 us (94%)
  local copies, waits for them, and re-layouts  13.8 us (4%)
  other arithmetic  5.79 us (2%)
    pallas_call x1, Pallas kernels, relay_body(): pl.pallas_call(relay_kernel, out_shape=jax.ShapeDtypeStruct((rows, cols),...  289 us

commit v1 on v0

--- a/solution.py
+++ b/solution.py
@@ -67,15 +67,15 @@
 
 MESH = pl.DeviceIdType.MESH
 LANES = 128
-CHUNKS = 4
+CHUNKS = 8
 HALVES = 2
 
 
 def relay_kernel(
     act, weight, shrink, expand, slots, out,
-    xp, ab, wv, sv, ev, mv, part, rsb, sh, spread, cs, rc, sx, rx, ov,
+    xp, ab, fb, stage, wv, sv, ev, mv, part, rsb, sh, spread, cs, rc, sx, rx, ov,
     load_sem, own_send, own_recv, fwd_send, fwd_recv, xown_send, xown_recv,
-    up_send, dn_send, flow_recv, rs_send, rs_recv, ag_send, ag_recv,
+    up_send, dn_send, flow_recv, f_send, f_recv, c_send, stage_sem, rs_send, rs_recv, ag_send, ag_recv,
     cs_send, cs_recv, x_send, x_recv, out_sem,
 ):
     x, p, z = lax.axis_index("dp"), lax.axis_index("pipe"), lax.axis_index("tensor")
@@ -103,7 +103,6 @@
 
     loads = [
         pltpu.make_async_copy(act, xp.at[d], load_sem.at[0]),
-        pltpu.make_async_copy(shrink, sv, load_sem.at[1]),
         pltpu.make_async_copy(slots, mv, load_sem.at[2]),
         pltpu.make_async_copy(weight, wv, load_sem.at[3]),
         pltpu.make_async_copy(expand, ev, load_sem.at[4]),
@@ -117,6 +116,21 @@
     pl.semaphore_signal(barrier, inc=1, device_id=other, device_id_type=MESH)
     pl.semaphore_wait(barrier, nz + 1)
     loads[0].wait()
+    pairs = shrink.shape[0] // 2
+
+    def stage_copy(i):
+        return pltpu.make_async_copy(
+            shrink.at[pl.ds(2 * i, 2)], stage.at[i % 2], stage_sem.at[i % 2]
+        )
+
+    stage_copy(0).start()
+    stage_copy(1).start()
+
+    def gather_pair(i):
+        stage_copy(i).wait()
+        sv[:, i * LANES:(i + 1) * LANES] = jnp.concatenate([stage[i % 2, 0], stage[i % 2, 1]], axis=1)
+        if i + 2 < pairs:
+            stage_copy(i + 2).start()
 
     def own_x(c):
         s = xp.at[d, cr(c)]
@@ -140,58 +154,99 @@
     up = (z >= d) & (z < nz - 1)
     dn = (z <= d) & (z > 0)
 
+    def goes(k, step):
+        if k != 2:
+            return up if step == 1 else dn
+        return (up & (x == 1)) if step == 1 else (dn & (x == 0))
+
     def send_flow(k, c, src):
-        @pl.when(up)
+        @pl.when(goes(k, 1))
         def _():
             flow(k, c, src, 1).start()
 
-        @pl.when(dn)
+        @pl.when(goes(k, -1))
         def _():
             flow(k, c, src, -1).start()
+
+    def arrive(k, c):
+        s = ab.at[blk(k), cr(c)]
+        rcopy(s, s, up_send.at[k, c], flow_recv.at[k, c], core).wait_recv()
 
     def relay(k, c):
         @pl.when(jnp.logical_not(origin))
         def _():
-            s = ab.at[blk(k), cr(c)]
-            rcopy(s, s, up_send.at[k, c], flow_recv.at[k, c], core).wait_recv()
+            arrive(k, c)
             send_flow(k, c, ab)
+
+    dx = blk(2)
+    f_origin = z == dx
+    f_member = ((x == 1) & (z > dx)) | ((x == 0) & (z < dx))
+    f_next = (f_origin | f_member) & (((x == 1) & (z < nz - 1)) | ((x == 0) & (z > 0)))
+
+    def f_copy(c, src):
+        return rcopy(src, fb.at[cr(c)], f_send.at[c], f_recv.at[c], {"tensor": z + 2 * x - 1})
+
+    def cross(c):
+        return rcopy(fb.at[cr(c)], ab.at[d, cr(c)], c_send.at[c], flow_recv.at[2, c], other)
+
+    def f_relay(c):
+        @pl.when(f_member)
+        def _():
+            s = fb.at[cr(c)]
+            rcopy(s, s, f_send.at[c], f_recv.at[c], core).wait_recv()
+
+            @pl.when(f_next)
+            def _():
+                f_copy(c, fb.at[cr(c)]).start()
+
+            cross(c).start()
 
     for c in range(CHUNKS):
         own_x(c).start()
         own_core(c).start()
 
-        @pl.when(origin)
-        def _():
+        @pl.when(f_origin & f_next)
+        def _():
+            f_copy(c, xp.at[d, cr(c)]).start()
+
+    def relays(c):
+        relay(1, c)
+        f_relay(c)
+        relay(3, c)
+
+    steps = CHUNKS // 2
+    for i in range(steps):
+        for c in (2 * i, 2 * i + 1):
+            own_core(c).wait_recv()
+
+            @pl.when(origin)
+            def _():
+                send_flow(1, c, xp)
+
+            own_x(c).wait_recv()
+            fwd(c).start()
+
+            @pl.when(origin)
+            def _():
+                send_flow(2, c, xp)
+
+            fwd(c).wait_recv()
+
+            @pl.when(origin)
+            def _():
+                send_flow(3, c, xp)
+
+        for g in range(i * pairs // steps, (i + 1) * pairs // steps):
+            gather_pair(g)
+        if i > 0:
+            relays(i - 1)
+
+    @pl.when(origin)
+    def _():
+        for c in range(CHUNKS):
             send_flow(0, c, xp)
 
-    for c in range(CHUNKS):
-        own_core(c).wait_recv()
-
-        @pl.when(origin)
-        def _():
-            send_flow(1, c, xp)
-
-        own_x(c).wait_recv()
-        fwd(c).start()
-
-        @pl.when(origin)
-        def _():
-            send_flow(2, c, xp)
-
-        if c > 0:
-            relay(0, c - 1)
-            relay(1, c - 1)
-        fwd(c).wait_recv()
-
-        @pl.when(origin)
-        def _():
-            send_flow(3, c, xp)
-
-    relay(0, CHUNKS - 1)
-    relay(1, CHUNKS - 1)
-
     loads[1].wait()
-    loads[2].wait()
     groups = sv.shape[1] // LANES
 
     def shrink_step(i, _):
@@ -216,10 +271,8 @@
 
     for j in range(1, nz):
         rs_copy(j).start()
-
-    for c in range(1):
-        relay(2, c)
-        relay(3, c)
+    relays(3)
+    relays(4)
     for j in range(1, nz):
         rs_copy(j).wait_recv()
     total = part[z].astype(jnp.float32)
@@ -228,12 +281,11 @@
     sh[z] = total.astype(jnp.bfloat16)
     for j in range(1, nz):
         ag_copy(j).start()
-    relay(2, 1)
-    relay(3, 1)
+    relays(5)
     for j in range(1, nz):
         ag_copy(j).wait_recv()
+    loads[2].wait()
     loads[3].wait()
-    loads[4].wait()
 
     @pl.when(origin)
     def _():
@@ -253,7 +305,7 @@
         def step(n, _):
             cols = pl.ds(pl.multiple_of(n * tile, tile), tile)
             value = jnp.dot(ab[b, hr(h), :], wv[:, cols], preferred_element_type=jnp.float32)
-            value += jnp.dot(spread[...], ev[:, cols], preferred_element_type=jnp.float32)
+            value += jnp.dot(spread[...], ev[:, :, cols].reshape(spread.shape[1], tile), preferred_element_type=jnp.float32)
             emit(value, cols)
             return 0
 
@@ -284,17 +336,31 @@
         compute(2, h, emit)
         x_copy(h).start()
 
-    for h in range(HALVES):
-        if h > 0:
-            for c in range(2 * h, 2 * h + 2):
-                relay(2, c)
-                relay(3, c)
-        to_core(1, 3, h)
-        if h == 0:
-            to_core(0, 1, 0)
-        to_x(h)
-        if h == 0:
-            to_core(0, 1, 1)
+    per = CHUNKS // HALVES
+
+    def arrive_half(h):
+        @pl.when(jnp.logical_not(origin))
+        def _():
+            for c in range(per * h, per * (h + 1)):
+                arrive(2, c)
+
+    to_core(1, 3, 0)
+    relays(6)
+    to_core(0, 1, 0)
+    relays(7)
+    to_core(1, 3, 1)
+    relay(0, 0)
+    relay(0, 1)
+    arrive_half(0)
+    to_x(0)
+    relay(0, 2)
+    relay(0, 3)
+    to_core(0, 1, 1)
+    relay(0, 4)
+    arrive_half(1)
+    to_x(1)
+    for c in range(5, CHUNKS):
+        relay(0, c)
 
     for h in range(HALVES):
         core_copy(0, h).wait_recv()
@@ -320,16 +386,24 @@
         own_x(c).wait_send()
         own_core(c).wait_send()
         fwd(c).wait_send()
-    for k in range(4):
-        for c in range(CHUNKS):
-
-            @pl.when(up)
+    for c in range(CHUNKS):
+        for k in range(4):
+
+            @pl.when(goes(k, 1))
             def _():
                 flow(k, c, ab, 1).wait_send()
 
-            @pl.when(dn)
+            @pl.when(goes(k, -1))
             def _():
                 flow(k, c, ab, -1).wait_send()
+
+        @pl.when(f_next)
+        def _():
+            f_copy(c, fb.at[cr(c)]).wait_send()
+
+        @pl.when(f_member)
+        def _():
+            cross(c).wait_send()
 
 
 def relay_body(
@@ -338,24 +412,17 @@
     rows, feats = activations.shape
     cols = query_weight.shape[1]
     shards = lax.axis_size(("dp", "pipe"))
-    reqs = offsets.shape[0] - 1
     held, _, rank = shrink_pages.shape
-    mine = reqs // shards
     shard = lax.axis_index(("dp", "pipe"))
     adapter_ids = jnp.arange(page_table.shape[0], dtype=jnp.int32)
     match = (request_adapter[:, None] == adapter_ids[None, :]).astype(jnp.int32)
     page_of_request = jnp.sum(match * page_table[None, :], axis=1)
-    lead = (shard - page_of_request[0] // held + shards) % shards
-    pages = page_of_request.reshape(mine, shards)
-    hot = (jnp.arange(shards, dtype=jnp.int32) == lead).astype(jnp.int32)
-    pages = jnp.clip(jnp.sum(pages * hot[None, :], axis=1) - shard * held, 0, held - 1)
     positions = jnp.arange(rows * shards, dtype=jnp.int32)
-    request = jnp.sum((offsets[None, 1:] <= positions[:, None]).astype(jnp.int32), axis=1)
-    slot = jnp.where(request % shards == lead, request // shards, -8)
+    inside = (offsets[None, :-1] <= positions[:, None]) & (positions[:, None] < offsets[None, 1:])
+    slot = jnp.sum(jnp.where(inside, page_of_request[None, :], 0), axis=1) - shard * held
+    slot = jnp.where((slot >= 0) & (slot < held), slot, -8)
     upper = (jnp.arange(LANES, dtype=jnp.int32) >= rank).astype(jnp.int32)
     slots = (slot[:, None] - upper[None, :]).reshape(shards, rows, LANES)
-    shrink = jnp.take(shrink_pages, pages, axis=0).transpose(1, 0, 2).reshape(feats, mine * rank)
-    expand = jnp.take(expand_pages, pages, axis=0).reshape(mine * rank, cols)
     bf, dma = jnp.bfloat16, pltpu.SemaphoreType.DMA
     hf = rows // HALVES
     nz = lax.axis_size("tensor")
@@ -367,14 +434,16 @@
         scratch_shapes=[
             pltpu.VMEM((shards, rows, feats), bf),
             pltpu.VMEM((shards, rows, feats), bf),
+            pltpu.VMEM((rows, feats), bf),
+            pltpu.VMEM((2, 2, feats, rank), bf),
             pltpu.VMEM(query_weight.shape, bf),
-            pltpu.VMEM(shrink.shape, bf),
-            pltpu.VMEM(expand.shape, bf),
+            pltpu.VMEM((feats, held * rank), bf),
+            pltpu.VMEM(expand_pages.shape, bf),
             pltpu.VMEM(slots.shape, jnp.int32),
             pltpu.VMEM((shards, rows, LANES), bf),
             pltpu.VMEM((nz - 1, rows, LANES), bf),
             pltpu.VMEM((shards, rows, LANES), bf),
-            pltpu.VMEM((hf, mine * rank), bf),
+            pltpu.VMEM((hf, held * rank), bf),
             pltpu.VMEM((2, rows, cols), bf),
             pltpu.VMEM((2, rows, cols), bf),
             pltpu.VMEM((rows, cols), bf),
@@ -383,16 +452,17 @@
             dma((6,)),
             dma((CHUNKS,)), dma((CHUNKS,)), dma((CHUNKS,)), dma((CHUNKS,)), dma((CHUNKS,)), dma((CHUNKS,)),
             dma((4, CHUNKS)), dma((4, CHUNKS)), dma((4, CHUNKS)),
+            dma((CHUNKS,)), dma((CHUNKS,)), dma((CHUNKS,)), dma((2,)),
             dma((nz - 1,)), dma((nz - 1,)), dma((nz - 1,)), dma((nz - 1,)),
             dma((2, HALVES)), dma((2, HALVES)), dma((HALVES,)), dma((HALVES,)), dma((HALVES,)),
         ],
         compiler_params=pltpu.CompilerParams(
-            collective_id=0, has_side_effects=True, vmem_limit_bytes=60 * 1024 * 1024
+            collective_id=0, has_side_effects=True, vmem_limit_bytes=62 * 1024 * 1024
         ),
         cost_estimate=pl.CostEstimate(
             flops=2 * shards * rows * feats * cols, bytes_accessed=2 * feats * cols, transcendentals=0
         ),
-    )(activations, query_weight, shrink, expand, slots)
+    )(activations, query_weight, shrink_pages, expand_pages, slots)
 
 
 def solution(mesh):

time: 309 us -> 259 us (0.84); the launches traced: 309 us -> 255 us
  Pallas kernels: 289 us -> 240 us
  other arithmetic: 5.79 us -> 2.38 us
    pallas_call x1, Pallas kernels: 289 us -> 240 us  [relay_body(): pl.pallas_call(relay_kernel, out_shape=jax.ShapeDtypeStruct((rows, cols),...]
    unnamed x1 -> x2, local copies, waits for them, and re-layouts: 3.16 us -> 11.5 us
    gather x2 -> x0, local copies, waits for them, and re-layouts: 5.73 us -> none  [the longest x1 2.87 us: relay_body(): jnp.take(shrink_pages, pages, axis=0).transpose(1, 0, 2)]
    reshape x2 -> x0, local copies, waits for them, and re-layouts: 4.01 us -> none  [the longest x1 3.93 us: relay_body(): jnp.take(shrink_pages, pages, axis=0).transpose(1, 0, 2)]
    select_n x4 -> x1, other arithmetic: 3.29 us -> 0.01 us  [relay_body(): slot = jnp.where((slot >= 0) & (slot < held), slot, -8)]
where the time goes in v1:
time: 259 us; the launch traced here: 255 us
  Pallas kernels  240 us (93%)
  local copies, waits for them, and re-layouts  12.3 us (5%)
    pallas_call x1, Pallas kernels, relay_body(): pl.pallas_call(relay_kernel, out_shape=jax.ShapeDtypeStruct((rows, cols),...  240 us
    unnamed x2, local copies, waits for them, and re-layouts  11.5 us

profile of v1, /device:TPU:0, one launch (start us, length us, event | category | flops | bytes accessed | tf_op | source)
XLA Modules:
  0.0 254.7 jit_solution(1379982476543707187)
XLA Ops:
  0.0 0.9 select_reduce_fusion.1
  0.9 0.8 fusion.1
  1.7 0.1 select_reduce_fusion
  1.9 1.3 broadcast_subtract_fusion.slots
  3.2 8.4 %copy.9.shrink = bf16[16,2048,64]{2,1,0:T(8,128)(2,1)} copy(bf16[16,2048,64]{1,2,0:T(8,128)(2,1)} %param.12) | data formatting | bytes 8388608 | tf_op args[5]
  11.6 240.0 %shard_map.73 = bf16[512,2048]{1,0:T(8,128)(2,1)} custom-call(bf16[512,2048]{1,0:T(8,128)(2,1)} %act.1, bf16[2048,2048]{1,0:T(8,128)(2,1)} %weight.1, bf16[16,2048,64]{2,1,0:T(8,128)(2,1)} %copy.9.shrink, bf16[16,64,2048]{2,1,0:T(8,128)(2,1)} %expand.1, s32[4,512,128]{2,1,0:T(8,128)} %broadcast_subtract_fusion.slots), custom_call_target="tpu_custom_call" | custom-call | flops 17179869184 | bytes 8388608 | tf_op jit(solution)/shard_map/pallas_call | solution.py:429
  251.6 3.2 %copy.11 = bf16[512,2048]{1,0:T(8,128)(2,1)} copy(bf16[512,2048]{1,0:T(8,128)(2,1)} %shard_map.73) | data formatting | bytes 4194304
  (4 shorter events, 0.0 us)

commit v2 on v1

--- a/solution.py
+++ b/solution.py
@@ -73,9 +73,9 @@
 
 def relay_kernel(
     act, weight, shrink, expand, slots, out,
-    xp, ab, fb, stage, wv, sv, ev, mv, part, rsb, sh, spread, cs, rc, sx, rx, ov,
+    xp, ab, fb, wv, sv, ev, mv, part, rsb, sh, spread, cs, rc, sx, rx, ov,
     load_sem, own_send, own_recv, fwd_send, fwd_recv, xown_send, xown_recv,
-    up_send, dn_send, flow_recv, f_send, f_recv, c_send, stage_sem, rs_send, rs_recv, ag_send, ag_recv,
+    up_send, dn_send, flow_recv, f_send, f_recv, c_send, rs_send, rs_recv, ag_send, ag_recv,
     cs_send, cs_recv, x_send, x_recv, out_sem,
 ):
     x, p, z = lax.axis_index("dp"), lax.axis_index("pipe"), lax.axis_index("tensor")
@@ -106,6 +106,7 @@
         pltpu.make_async_copy(slots, mv, load_sem.at[2]),
         pltpu.make_async_copy(weight, wv, load_sem.at[3]),
         pltpu.make_async_copy(expand, ev, load_sem.at[4]),
+        pltpu.make_async_copy(shrink, sv, load_sem.at[1]),
     ]
     for cp in loads:
         cp.start()
@@ -116,21 +117,6 @@
     pl.semaphore_signal(barrier, inc=1, device_id=other, device_id_type=MESH)
     pl.semaphore_wait(barrier, nz + 1)
     loads[0].wait()
-    pairs = shrink.shape[0] // 2
-
-    def stage_copy(i):
-        return pltpu.make_async_copy(
-            shrink.at[pl.ds(2 * i, 2)], stage.at[i % 2], stage_sem.at[i % 2]
-        )
-
-    stage_copy(0).start()
-    stage_copy(1).start()
-
-    def gather_pair(i):
-        stage_copy(i).wait()
-        sv[:, i * LANES:(i + 1) * LANES] = jnp.concatenate([stage[i % 2, 0], stage[i % 2, 1]], axis=1)
-        if i + 2 < pairs:
-            stage_copy(i + 2).start()
 
     def own_x(c):
         s = xp.at[d, cr(c)]
@@ -209,20 +195,34 @@
         def _():
             f_copy(c, xp.at[d, cr(c)]).start()
 
-    def relays(c):
-        relay(1, c)
-        f_relay(c)
-        relay(3, c)
+        @pl.when(origin)
+        def _():
+            send_flow(0, c, xp)
+
+    groups = shrink.shape[0] * shrink.shape[1] // LANES
+    half = LANES // 2
+
+    def shrink_block(k):
+        b = blk(k)
+        folded = []
+        for h in range(HALVES):
+            m = mv[b, hr(h), :]
+
+            def add(q, total):
+                pair = sv[pl.ds(4 * q, 4)].reshape(2 * LANES, sv.shape[2])
+                scores = lax.dot_general(
+                    xp[b, hr(h), :], pair, (((1,), (1,)), ((), ())), preferred_element_type=jnp.float32
+                )
+                total += jnp.where(m == 4 * q, scores[:, :LANES], 0.0)
+                return total + jnp.where(m == 4 * q + 2, scores[:, LANES:], 0.0)
+
+            total = lax.fori_loop(0, groups // 2, add, jnp.zeros((hf, LANES), jnp.float32))
+            folded.append(total[:, :half] + total[:, half:])
+        part[b] = jnp.concatenate(folded, axis=1).astype(jnp.bfloat16)
 
     steps = CHUNKS // 2
     for i in range(steps):
         for c in (2 * i, 2 * i + 1):
-            own_core(c).wait_recv()
-
-            @pl.when(origin)
-            def _():
-                send_flow(1, c, xp)
-
             own_x(c).wait_recv()
             fwd(c).start()
 
@@ -230,36 +230,35 @@
             def _():
                 send_flow(2, c, xp)
 
-            fwd(c).wait_recv()
-
-            @pl.when(origin)
-            def _():
-                send_flow(3, c, xp)
-
-        for g in range(i * pairs // steps, (i + 1) * pairs // steps):
-            gather_pair(g)
+        if i == 0:
+            loads[1].wait()
+            loads[4].wait()
+            shrink_block(0)
+        if i == 1:
+            for c in range(CHUNKS):
+                own_core(c).wait_recv()
+            shrink_block(1)
         if i > 0:
-            relays(i - 1)
+            for c in (2 * i - 2, 2 * i - 1):
+                relay(0, c)
+                f_relay(c)
+    for c in range(CHUNKS):
+        fwd(c).wait_recv()
+
+        @pl.when(origin)
+        def _():
+            send_flow(3, c, xp)
 
     @pl.when(origin)
     def _():
         for c in range(CHUNKS):
-            send_flow(0, c, xp)
-
-    loads[1].wait()
-    groups = sv.shape[1] // LANES
-
-    def shrink_step(i, _):
-        b, r = i // HALVES, pl.ds(pl.multiple_of((i % HALVES) * hf, hf), hf)
-        scores = jnp.dot(xp[b, r, :], sv[...], preferred_element_type=jnp.float32)
-        m = mv[b, r, :]
-        total = jnp.zeros((hf, LANES), jnp.float32)
-        for g in range(groups):
-            total += jnp.where(m == 2 * g, scores[:, g * LANES:(g + 1) * LANES], 0.0)
-        part[b, r, :] = total.astype(jnp.bfloat16)
-        return 0
-
-    lax.fori_loop(0, nz * HALVES, shrink_step, 0)
+            send_flow(1, c, xp)
+
+    shrink_block(2)
+    for c in (CHUNKS - 2, CHUNKS - 1):
+        relay(0, c)
+        f_relay(c)
+    shrink_block(3)
 
     def rs_copy(j):
         to = lax.rem(z + j, nz)
@@ -271,8 +270,8 @@
 
     for j in range(1, nz):
         rs_copy(j).start()
-    relays(3)
-    relays(4)
+    relay(3, 0)
+    relay(3, 1)
     for j in range(1, nz):
         rs_copy(j).wait_recv()
     total = part[z].astype(jnp.float32)
@@ -281,7 +280,8 @@
     sh[z] = total.astype(jnp.bfloat16)
     for j in range(1, nz):
         ag_copy(j).start()
-    relays(5)
+    relay(3, 2)
+    relay(3, 3)
     for j in range(1, nz):
         ag_copy(j).wait_recv()
     loads[2].wait()
@@ -298,7 +298,8 @@
     def compute(k, h, emit):
         b = blk(k)
         m = mv[b, hr(h), :]
-        s = sh[b, hr(h), :]
+        s = sh[b][:, h * half:(h + 1) * half]
+        s = jnp.concatenate([s, s], axis=1)
         for g in range(groups):
             spread[:, g * LANES:(g + 1) * LANES] = jnp.where(m == 2 * g, s, jnp.zeros_like(s))
 
@@ -344,27 +345,8 @@
             for c in range(per * h, per * (h + 1)):
                 arrive(2, c)
 
-    to_core(1, 3, 0)
-    relays(6)
-    to_core(0, 1, 0)
-    relays(7)
-    to_core(1, 3, 1)
-    relay(0, 0)
-    relay(0, 1)
-    arrive_half(0)
-    to_x(0)
-    relay(0, 2)
-    relay(0, 3)
-    to_core(0, 1, 1)
-    relay(0, 4)
-    arrive_half(1)
-    to_x(1)
-    for c in range(5, CHUNKS):
-        relay(0, c)
-
-    for h in range(HALVES):
+    def final(h):
         core_copy(0, h).wait_recv()
-
         x_copy(h).wait_recv()
 
         def emit(value, cols):
@@ -373,6 +355,27 @@
 
         compute(0, h, emit)
         out_copy(h).start()
+
+    def relay_pair(k, i):
+        relay(k, 2 * i)
+        relay(k, 2 * i + 1)
+
+    to_core(1, 3, 0)
+    relay_pair(3, 2)
+    arrive_half(0)
+    to_x(0)
+    relay_pair(3, 3)
+    to_core(1, 3, 1)
+    relay_pair(1, 0)
+    arrive_half(1)
+    to_x(1)
+    relay_pair(1, 1)
+    to_core(0, 1, 0)
+    relay_pair(1, 2)
+    final(0)
+    relay_pair(1, 3)
+    to_core(0, 1, 1)
+    final(1)
 
     for h in range(HALVES):
         out_copy(h).wait()
@@ -435,14 +438,13 @@
             pltpu.VMEM((shards, rows, feats), bf),
             pltpu.VMEM((shards, rows, feats), bf),
             pltpu.VMEM((rows, feats), bf),
-            pltpu.VMEM((2, 2, feats, rank), bf),
             pltpu.VMEM(query_weight.shape, bf),
-            pltpu.VMEM((feats, held * rank), bf),
+            pltpu.VMEM((held, rank, feats), bf),
             pltpu.VMEM(expand_pages.shape, bf),
             pltpu.VMEM(slots.shape, jnp.int32),
-            pltpu.VMEM((shards, rows, LANES), bf),
-            pltpu.VMEM((nz - 1, rows, LANES), bf),
-            pltpu.VMEM((shards, rows, LANES), bf),
+            pltpu.VMEM((shards, rows // 2, LANES), bf),
+            pltpu.VMEM((nz - 1, rows // 2, LANES), bf),
+            pltpu.VMEM((shards, rows // 2, LANES), bf),
             pltpu.VMEM((hf, held * rank), bf),
             pltpu.VMEM((2, rows, cols), bf),
             pltpu.VMEM((2, rows, cols), bf),
@@ -452,7 +454,7 @@
             dma((6,)),
             dma((CHUNKS,)), dma((CHUNKS,)), dma((CHUNKS,)), dma((CHUNKS,)), dma((CHUNKS,)), dma((CHUNKS,)),
             dma((4, CHUNKS)), dma((4, CHUNKS)), dma((4, CHUNKS)),
-            dma((CHUNKS,)), dma((CHUNKS,)), dma((CHUNKS,)), dma((2,)),
+            dma((CHUNKS,)), dma((CHUNKS,)), dma((CHUNKS,)),
             dma((nz - 1,)), dma((nz - 1,)), dma((nz - 1,)), dma((nz - 1,)),
             dma((2, HALVES)), dma((2, HALVES)), dma((HALVES,)), dma((HALVES,)), dma((HALVES,)),
         ],
@@ -462,7 +464,7 @@
         cost_estimate=pl.CostEstimate(
             flops=2 * shards * rows * feats * cols, bytes_accessed=2 * feats * cols, transcendentals=0
         ),
-    )(activations, query_weight, shrink_pages, expand_pages, slots)
+    )(activations, query_weight, shrink_pages.transpose(0, 2, 1), expand_pages, slots)
 
 
 def solution(mesh):

time: 259 us -> 247 us (0.954)
  the two profiles are of different devices: /device:TPU:0 before, /device:TPU:6 now
where the time goes in v2:
time: 247 us
  Pallas kernels  240 us (97%)
  local copies, waits for them, and re-layouts  3.97 us (2%)
    pallas_call x1, Pallas kernels, relay_body(): pl.pallas_call(relay_kernel, out_shape=jax.ShapeDtypeStruct((rows, cols),...  240 us

profile of v2, /device:TPU:6, one launch (start us, length us, event | category | flops | bytes accessed | tf_op | source)
XLA Modules:
  0.0 246.6 jit_solution(8929940537847274550)
XLA Ops:
  0.0 0.9 select_reduce_fusion.1
  0.9 0.8 fusion.1
  1.7 0.1 select_reduce_fusion
  1.9 1.3 broadcast_subtract_fusion.slots
  3.2 240.2 %shard_map.73 = bf16[512,2048]{1,0:T(8,128)(2,1)} custom-call(bf16[512,2048]{1,0:T(8,128)(2,1)} %act.1, bf16[2048,2048]{1,0:T(8,128)(2,1)} %weight.1, bf16[16,64,2048]{2,1,0:T(8,128)(2,1)} %bitcast.1, bf16[16,64,2048]{2,1,0:T(8,128)(2,1)} %expand.1, s32[4,512,128]{2,1,0:T(8,128)} %broadcast_subtract_fusion.slots), custom_call_target="tpu_custom_call" | custom-call | flops 17179869184 | bytes 8388608 | tf_op jit(solution)/shard_map/pallas_call | solution.py:432
  243.4 3.2 %copy.9 = bf16[512,2048]{1,0:T(8,128)(2,1)} copy(bf16[512,2048]{1,0:T(8,128)(2,1)} %shard_map.73) | data formatting | bytes 4194304
  (4 shorter events, 0.0 us)
